TPU v7x, 32 devices: a whole 2x2x4 slice. The times are simulated.
32 devices in a mesh: dom: 2 (over x), tok: 16 (over z, y, core).
Axes of the slice: x: 2, y: 2, z: 4, core: 2. Of those that a mesh axis runs over, the one named last changes fastest.
Arguments:
- tokens: bfloat16 [512, 4096], P(('dom', 'tok')), parts along dimension 0, may hold values from -6 to 6
- rotation_flip: int32 [4096], replicated, may hold values from 0 to 1
- gate_up: bfloat16 [4, 4096, 16384], P('dom', None, 'tok'), parts along dimension 0, may hold values from -0.09375 to 0.09375
- quant_codes: bfloat16 [4, 4096, 16384], P('dom', None, 'tok'), parts along dimension 0, may hold values from -7 to 7
- quant_exps: int32 [4, 32, 16384], P('dom', None, 'tok'), parts along dimension 0, may hold values from -10 to -7
- down_rows: bfloat16 [32768, 4096], P(('dom', 'tok')), parts along dimension 0, may hold values from -0.046875 to 0.046875
Outputs:
- correction: bfloat16 [32768, 4096], P(('dom', 'tok')), parts along dimension 0
There are 2 independent parts, one for each index of `dom`. A program takes and returns all parts, laid end to end along the dimension named above; an argument that names none is the same for every part. Nothing has to cross between parts.
All inputs are finite; a program needn't handle non-finite values.
Results may differ from a plain program's by a relative error of at most 0.012.
Values may be sent and summed in bfloat16 or wider, within the bound.
A program may use at most 128 MiB of HBM per device.

v0:
```python
import jax
import jax.numpy as jnp
from jax import lax
from jax.sharding import PartitionSpec as P


def hadamard_table(order):
    index = jnp.arange(order, dtype=jnp.int32)
    common = index[:, None] & index[None, :]
    parity = jnp.zeros((order, order), jnp.int32)
    for bit_pos in range(max(order.bit_length() - 1, 1)):
        parity = parity ^ common >> bit_pos & 1
    return (1 - 2 * parity).astype(jnp.float32)


def rotate(inputs, flip):
    width = inputs.shape[-1]
    signed = inputs.astype(jnp.float32) * (1 - 2 * flip).astype(jnp.float32)
    power = width.bit_length() - 1
    outer_len = 2 ** (power // 2)
    inner_len = width // outer_len
    blocks = signed.reshape(-1, outer_len, inner_len)
    mixed = jnp.einsum(
        "ab,nbc,cd->nad",
        hadamard_table(outer_len),
        blocks,
        hadamard_table(inner_len),
        precision=lax.Precision.HIGHEST,
    )
    return (mixed.reshape(-1, width) * (1.0 / width**0.5)).astype(jnp.bfloat16)


def dequant(codes, exps):
    groups = exps.shape[1]
    scales = jnp.exp2(exps.astype(jnp.float32))
    shaped = codes.astype(jnp.float32).reshape(2, groups, codes.shape[1] // groups, codes.shape[2])
    return (shaped * scales[:, :, None, :]).reshape(codes.shape).astype(jnp.bfloat16)


def swiglu(inputs, weights):
    gate = jnp.dot(inputs, weights[0], preferred_element_type=jnp.float32)
    upper = jnp.dot(inputs, weights[1], preferred_element_type=jnp.float32)
    return (jax.nn.silu(gate) * upper).astype(jnp.bfloat16)


def per_device(tokens, rotation_flip, gate_up, quant_codes, quant_exps, down_rows):
    quant_weight = dequant(quant_codes, quant_exps)
    piece = lax.all_gather(tokens, "tok", axis=0, tiled=True)
    hid_full = swiglu(piece, gate_up)
    hid_quant = swiglu(rotate(piece, rotation_flip), quant_weight)
    mismatch = (hid_full.astype(jnp.float32) - hid_quant.astype(jnp.float32)).astype(jnp.bfloat16)
    total_tokens = mismatch.shape[0]
    partial_proj = jnp.dot(mismatch, down_rows, preferred_element_type=jnp.float32)
    projected = lax.psum(partial_proj, "tok").astype(jnp.bfloat16)
    gram = lax.dot_general(
        hid_quant, projected, (((0,), (0,)), ((), ())), preferred_element_type=jnp.float32
    )
    return (gram * (1.0 / total_tokens**0.5)).astype(jnp.bfloat16)


def solution(mesh):
    placed = (
        P(("dom", "tok"), None),
        P(),
        P("dom", None, "tok"),
        P("dom", None, "tok"),
        P("dom", None, "tok"),
        P(("dom", "tok"), None),
    )
    return jax.shard_map(
        per_device, mesh=mesh, in_specs=placed, out_specs=P(("dom", "tok"), None), check_vma=False
    )
```

profile of v0, /device:TPU:1, one launch (start us, length us, event | category | flops | bytes accessed | tf_op | source)
XLA Modules:
  0.0 202.9 jit_solution(15538142856855820026)
XLA Ops:
  6.5 0.0 all-gather.2.cloned.1.call-start
  6.5 0.7 all-gather.2.cloned.1.call-update
  7.3 1.0 multiply_exponential_fusion
  8.3 0.0 copy-start.2
  8.3 14.8 %fusion = bf16[2,4096,1024]{2,1,0:T(8,128)(2,1)} fusion(bf16[2,4096,1024]{2,1,0:T(8,128)(2,1)} %param.9, f32[2,32,1024]{2,1,0:T(8,128)S(1)} %multiply_exponential_fusion), kind=kLoop, calls=%fused_computation.1 | loop fusion | flops 25165824 | bytes 33816576 | tf_op jit(solution)/shard_map/convert_element_type | solution.py:37
  23.1 0.0 copy-done.2
  23.1 30.4 %all-gather.2.cloned.1.call-done = bf16[256,4096]{1,0:T(8,128)(2,1)} async-done(((bf16[16,4096]{1,0:T(8,128)(2,1)}), bf16[256,4096]{1,0:T(8,128)(2,1)}) %all-gather.2.cloned.1.call-update) | async-done | bytes 2097168 | tf_op jit(solution)/shard_map/all_gather | solution.py:48
  53.5 3.3 %copy.8 = bf16[256,4096]{0,1:T(8,128)(2,1)S(1)} copy(bf16[256,4096]{1,0:T(8,128)(2,1)} %all-gather.2.cloned.1.call-done) | data formatting | bytes 4194304 | tf_op jit(solution)/shard_map/all_gather | solution.py:48
  56.7 0.0 copy-start
  56.7 0.7 convert_multiply_fusion
  57.5 6.8 %fusion.11 = f32[256,64,64]{0,2,1:T(8,128)S(1)} fusion(f32[256,64,64]{0,2,1:T(8,128)S(1)} %bitcast.47), kind=kOutput, calls=%fused_computation.15 | convolution fusion | flops 805392384 | bytes 8388608 | tf_op jit(solution)/shard_map/ab,nbc,cd->nad/dot_general | solution.py:23
  64.2 6.0 %multiply_convert_fusion.1 = bf16[256,64,64]{0,2,1:T(8,128)(2,1)S(1)} fusion(f32[256,64,64]{0,2,1:T(8,128)S(1)} %fusion.11), kind=kOutput, calls=%fused_computation.17 | convolution fusion | flops 807489536 | bytes 6291456 | tf_op jit(solution)/shard_map/ab,nbc,cd->nad/dot_general | solution.py:23
  70.3 0.0 copy-done
  70.3 2.4 %fusion.2 = f32[256,1024]{1,0:T(8,128)S(1)} fusion(bf16[256,4096]{0,1:T(8,128)(2,1)S(1)} %bitcast.48, bf16[2,4096,1024]{2,1,0:T(8,128)(2,1)S(1)} %copy-done), kind=kOutput, calls=%fused_computation.6 | convolution fusion | flops 2147483648 | bytes 11534336 | tf_op jit(solution)/shard_map/dot_general | solution.py:41
  72.6 0.0 copy-start.1
  72.7 2.4 %fusion.20 = bf16[256,1024]{1,0:T(8,128)(2,1)S(1)} fusion(bf16[256,4096]{0,1:T(8,128)(2,1)S(1)} %bitcast.49, bf16[2,4096,1024]{2,1,0:T(8,128)(2,1)S(1)} %copy-done, f32[256,1024]{1,0:T(8,128)S(1)} %fusion.2), kind=kOutput, calls=%fused_computation.22 | convolution fusion | flops 2149056512 | bytes 12058624 | tf_op jit(solution)/shard_map/dot_general | solution.py:42
  75.1 0.0 copy-done.1
  75.1 6.7 %fusion.5 = f32[256,1024]{1,0:T(8,128)} fusion(bf16[256,4096]{1,0:T(8,128)(2,1)S(1)} %copy-done.1, bf16[2,4096,1024]{2,1,0:T(8,128)(2,1)} %param.8), kind=kOutput, calls=%fused_computation.9 | convolution fusion | flops 2147483648 | bytes 11534336 | tf_op jit(solution)/shard_map/dot_general | solution.py:41
  81.8 12.7 %fusion.34 = f32[256,4096]{1,0:T(8,128)} fusion(bf16[1024,4096]{1,0:T(8,128)(2,1)} %param.11, bf16[256,4096]{1,0:T(8,128)(2,1)S(1)} %copy-done.1, bf16[2,4096,1024]{2,1,0:T(8,128)(2,1)} %param.8, bf16[256,1024]{1,0:T(8,128)(2,1)S(1)} %fusion.20, f32[256,1024]{1,0:T(8,128)} %fusion.5), kind=kOutput, calls=%fused_computation.27 | convolution fusion | flops 4297588736 | bytes 24641536 | tf_op jit(solution)/shard_map/dot_general | solution.py:53
  94.5 95.8 %all-reduce.1 = bf16[256,4096]{1,0:T(8,128)(2,1)S(1)} all-reduce(f32[256,4096]{1,0:T(8,128)} %fusion.34), channel_id=1, replica_groups=mesh['dom'=2,'tok'=16] {'tok'}, use_global_device_ids=true, to_apply=%region_0.1 | all-reduce | flops 1048576 | bytes 6291456 | tf_op jit(solution)/shard_map/psum | solution.py:54
  190.3 5.8 %multiply_convert_fusion = bf16[1024,4096]{1,0:T(8,128)(2,1)} fusion(bf16[256,1024]{1,0:T(8,128)(2,1)S(1)} %fusion.20, bf16[256,4096]{1,0:T(8,128)(2,1)S(1)} %all-reduce.1), kind=kOutput, calls=%fused_computation.2 | convolution fusion | flops 2155872256 | bytes 11010048 | tf_op jit(solution)/shard_map/dot_general | solution.py:55
  (1 shorter events, 0.0 us)
Async XLA Ops:
  6.5 46.9 %all-gather.2.cloned.1.call-start = ((), (), s32[]{:S(2)}) async-start(), calls=%async_computation | async-start | bytes 2228224 | tf_op jit(solution)/shard_map/all_gather | solution.py:48
  8.3 14.8 %copy-start.2 = (s32[4096]{0:T(1024)S(1)}, s32[4096]{0:T(1024)}, u32[]{:S(2)}) copy-start(s32[4096]{0:T(1024)} %param.7) | copy-start | bytes 49156
  56.7 13.5 %copy-start = (bf16[2,4096,1024]{2,1,0:T(8,128)(2,1)S(1)}, bf16[2,4096,1024]{2,1,0:T(8,128)(2,1)}, u32[]{:S(2)}) copy-start(bf16[2,4096,1024]{2,1,0:T(8,128)(2,1)} %fusion) | copy-start | bytes 50331652
  72.6 2.5 %copy-start.1 = (bf16[256,4096]{1,0:T(8,128)(2,1)S(1)}, bf16[256,4096]{1,0:T(8,128)(2,1)}, u32[]{:S(2)}) copy-start(bf16[256,4096]{1,0:T(8,128)(2,1)} %all-gather.2.cloned.1.call-done) | copy-start | bytes 6291460
Sparse Core Ops, SparseCore 0:
  9.5 43.8 all-gather.1
where the time goes:
time: 203 us
  blocking collectives  95.8 us (47%)
  matrix products  42.8 us (21%)
  waiting for transfers between devices  31.1 us (15%)
  other arithmetic  16.5 us (8%)
  between operations  13.5 us (7%)
  local copies, waits for them, and re-layouts  3.28 us (2%)
    psum x1, blocking collectives, per_device(): projected = lax.psum(partial_proj, 'tok').astype(jnp.bfloat16)  95.8 us
    all_gather x1, waiting for transfers between devices, per_device(): piece = lax.all_gather(tokens, 'tok', axis=0, tiled=True)  30.4 us
    convert_element_type x1, other arithmetic, dequant(): (shaped * scales[:, :, None, :]).reshape(codes.shape).astype(jnp.bfloat16)  14.8 us
    dot_general x2, matrix products, rotate(): jnp.einsum('ab,nbc,cd->nad', hadamard_table(outer_len), blocks, hadamard_...  12.8 us
    dot_general x1, matrix products, per_device(): jnp.dot(mismatch, down_rows, preferred_element_type=jnp.float32)  12.7 us
    dot_general x2, matrix products, swiglu(): gate = jnp.dot(inputs, weights[0], preferred_element_type=jnp.float32)  9.03 us
    dot_general x1, matrix products, per_device(): lax.dot_general(hid_quant, projected, (((0,), (0,)), ((), ())), preferred...  5.79 us
  transfers between devices with their start and end apart: 1, of which 1 were waited for; matrix products, arithmetic and copies ran while one was open for 8% of the time, Pallas kernels for 0%

commit v1 on v0

v1 whole, which is shorter than its diff:
```python
import functools

import jax
import jax.numpy as jnp
import numpy as np
from jax import lax
from jax.experimental import pallas as pl
from jax.experimental.pallas import tpu as pltpu
from jax.sharding import PartitionSpec as P

MESH = pl.DeviceIdType.MESH
F32 = jnp.float32
BF16 = jnp.bfloat16


def hadamard_block(order):
    index = np.arange(order)
    common = index[:, None] & index[None, :]
    parity = np.zeros((order, order), np.int32)
    for bit_pos in range(order.bit_length()):
        parity ^= (common >> bit_pos) & 1
    return (1 - 2 * parity).astype(np.float32)


def xor(value, mask):
    out, bit = value, 1
    while bit <= mask:
        if mask & bit:
            out = out + bit * (1 - 2 * ((value // bit) % 2))
        bit *= 2
    return out


def kernel(
    n, group,
    tok_ref, flip_ref, had_ref, exps_ref, gu_hbm, codes_hbm, down_hbm,
    hidq_ref, proj_hbm,
    gu_v, codes_v, down_v, tok_v, rot_v, mis_v, proj_v,
    csend, crecv, ysend, yrecv, zsend, zrecv,
    codes_sem, gu_sem, down_sem, out_sem,
    az_s, az_r, ay_s, ay_r, ac_s, ac_r,
    bz_s, bz_r, by_s, by_r, bc_s, bc_r,
    rz_s, rz_r, ry_s, ry_r, rc_s, rc_r,
):
    nz = n // 4
    me = lax.axis_index("tok")
    z, y, c = me // 4, (me // 2) % 2, me % 2
    own_rows, width = tok_ref.shape
    tokens = own_rows * n
    hidden = mis_v.shape[1]
    cols = proj_v.shape[1] // n

    def index(zz, yy, cc):
        return (zz * 2 + yy) * 2 + cc

    zs = [xor(z, k) for k in range(nz)]
    z_peer = [index(zs[k], y, c) for k in range(nz)]
    y_peer, c_peer = index(z, 1 - y, c), index(z, y, 1 - c)

    chunks = codes_sem.shape[1]
    depth = width // chunks
    code_copies = [
        pltpu.make_async_copy(
            codes_hbm.at[p, pl.ds(q * depth, depth)],
            codes_v.at[p, pl.ds(q * depth, depth)],
            codes_sem.at[p, q],
        )
        for p in range(2) for q in range(chunks)
    ]
    gu_copies = [
        pltpu.make_async_copy(gu_hbm.at[p], gu_v.at[p], gu_sem.at[p]) for p in range(2)
    ]
    down_copy = pltpu.make_async_copy(down_hbm, down_v, down_sem)
    for copy in code_copies + gu_copies + [down_copy]:
        copy.start()

    def row_block(i):
        return tok_v.at[pl.ds(pl.multiple_of(i * own_rows, own_rows), own_rows)]

    def col_block(i):
        return proj_v.at[:, pl.ds(pl.multiple_of(i * cols, cols), cols)]

    row_block(me)[...] = tok_ref[...]

    barrier = pltpu.get_barrier_semaphore()
    peers = z_peer[1:] + [y_peer, c_peer]
    for peer in peers:
        pl.semaphore_signal(barrier, inc=1, device_id={"tok": peer}, device_id_type=MESH)
    pl.semaphore_wait(barrier, len(peers))

    sent = []

    def send(src, dst, ssem, rsem, peer):
        copy = pltpu.make_async_remote_copy(
            src_ref=src, dst_ref=dst, send_sem=ssem, recv_sem=rsem,
            device_id={"tok": peer}, device_id_type=MESH,
        )
        copy.start()
        sent.append(copy)

    def arrived(dst, ssem, rsem, peer):
        pltpu.make_async_remote_copy(
            src_ref=dst, dst_ref=dst, send_sem=ssem, recv_sem=rsem,
            device_id={"tok": peer}, device_id_type=MESH,
        ).wait_recv()

    def gather(block, sems, between, landed):
        z_s, z_r, y_s, y_r, c_s, c_r = sems

        def on_y(k):
            i = index(zs[k], 1 - y, c)
            arrived(block(i), y_s.at[k], y_r.at[k], y_peer)
            send(block(i), block(i), c_s.at[k, 1], c_r.at[k, 1], c_peer)
            landed(i)

        def out(k):
            i = z_peer[k]
            send(block(i), block(i), y_s.at[k], y_r.at[k], y_peer)
            send(block(i), block(i), c_s.at[k, 0], c_r.at[k, 0], c_peer)
            landed(i)

        for k in range(nz - 1, 0, -1):
            send(block(me), block(me), z_s.at[k], z_r.at[k], z_peer[k])
        out(0)
        between(0)
        for k in range(1, nz):
            arrived(block(z_peer[k]), z_s.at[k], z_r.at[k], z_peer[k])
            out(k)
            on_y(k - 1)
            between(k)
        on_y(nz - 1)
        for k in range(nz):
            for s in range(2):
                i = index(zs[k], y + s * (1 - 2 * y), 1 - c)
                arrived(block(i), c_s.at[k, s], c_r.at[k, s], c_peer)
                landed(i)

    def scale_chunk(t):
        p, q = t // chunks, t % chunks
        code_copies[t].wait()

        def one(step, carry):
            g = q * (depth // group) + step
            scale = jnp.exp2(exps_ref[p, pl.ds(g, 1), :].astype(F32))
            tile = jnp.broadcast_to(scale, (16, hidden)).astype(BF16)
            for r in range(group // 16):
                rows = pl.ds(pl.multiple_of(g * group + r * 16, 16), 16)
                codes_v[p, rows, :] = codes_v[p, rows, :] * tile
            return carry

        lax.fori_loop(0, depth // group, one, 0)

    total = 2 * chunks
    marks = [total // 2 + (total - total // 2) * k // (nz - 1) for k in range(nz)]

    def between(k):
        for t in range(marks[k - 1] if k else 0, marks[k]):
            scale_chunk(t)

    gather(row_block, (az_s, az_r, ay_s, ay_r, ac_s, ac_r), between, lambda i: None)

    had = had_ref.shape[0]
    sign = (1 - 2 * flip_ref[...]).astype(F32).astype(BF16)
    table = had_ref[...]
    span = min(64, tokens)

    def rotate(step, carry):
        rows = pl.ds(pl.multiple_of(step * span, span), span)
        parts = []
        for b in range(width // had):
            lanes = slice(b * had, (b + 1) * had)
            signed = tok_v[rows, lanes] * sign[:, lanes]
            parts.append(jnp.dot(signed, table, preferred_element_type=F32))
        half = 1
        while half < len(parts):
            for b in range(len(parts)):
                if not b & half:
                    low, high = parts[b], parts[b + half]
                    parts[b], parts[b + half] = low + high, low - high
            half *= 2
        for b in range(width // had):
            rot_v[rows, b * had:(b + 1) * had] = (parts[b] * (1.0 / width**0.5)).astype(BF16)
        return carry

    lax.fori_loop(0, tokens // span, rotate, 0)

    for copy in gu_copies:
        copy.wait()
    tile = 256

    def swiglu(lhs, w, lanes):
        gate = jnp.dot(lhs[...], w[0, :, lanes], preferred_element_type=F32)
        upper = jnp.dot(lhs[...], w[1, :, lanes], preferred_element_type=F32)
        return (gate / (1.0 + jnp.exp(-gate)) * upper).astype(BF16)

    def hidden_tile(step, carry):
        lanes = pl.ds(pl.multiple_of(step * tile, tile), tile)
        full = swiglu(tok_v, gu_v, lanes)
        quant = swiglu(rot_v, codes_v, lanes)
        hidq_ref[:, lanes] = quant
        mis_v[:, lanes] = (full.astype(F32) - quant.astype(F32)).astype(BF16)
        return carry

    lax.fori_loop(0, hidden // tile, hidden_tile, 0)

    down_copy.wait()

    def partial(i):
        lanes = pl.ds(pl.multiple_of(i * cols, cols), cols)
        return jnp.dot(mis_v[...], down_v[:, lanes], preferred_element_type=F32)

    order = list(range(nz - 1, -1, -1))

    def to_core(k, s):
        yy = y + s * (1 - 2 * y)
        csend[k, s] = partial(index(zs[k], yy, 1 - c)).astype(BF16)
        send(csend.at[k, s], crecv.at[k, s], rc_s.at[k, s], rc_r.at[k, s], c_peer)

    def with_core(k, s):
        yy = y + s * (1 - 2 * y)
        mine = partial(index(zs[k], yy, c))
        arrived(crecv.at[k, s], rc_s.at[k, s], rc_r.at[k, s], c_peer)
        return mine + crecv[k, s].astype(F32)

    def with_y(k):
        mine = with_core(k, 0)
        arrived(yrecv.at[k], ry_s.at[k], ry_r.at[k], y_peer)
        return mine + yrecv[k].astype(F32)

    for k in order:
        to_core(k, 1)
    for k in order:
        ysend[k] = with_core(k, 1).astype(BF16)
        send(ysend.at[k], yrecv.at[k], ry_s.at[k], ry_r.at[k], y_peer)
    for k in order:
        to_core(k, 0)
    for k in order[:-1]:
        zsend[k] = with_y(k).astype(BF16)
        send(zsend.at[k], zrecv.at[k], rz_s.at[k], rz_r.at[k], z_peer[k])
    mine = with_y(0)
    for k in range(1, nz):
        arrived(zrecv.at[k], rz_s.at[k], rz_r.at[k], z_peer[k])
        mine = mine + zrecv[k].astype(F32)
    col_block(me)[...] = mine.astype(BF16)

    gather(col_block, (bz_s, bz_r, by_s, by_r, bc_s, bc_r), lambda k: None, lambda i: None)
    out_copy = pltpu.make_async_copy(proj_v, proj_hbm, out_sem)
    out_copy.start()
    for copy in sent:
        copy.wait_send()
    out_copy.wait()


def per_device(n, tokens, rotation_flip, gate_up, quant_codes, quant_exps, down_rows):
    own_rows, width = tokens.shape
    count = own_rows * n
    hidden, out_width = down_rows.shape
    group = width // quant_exps.shape[1]
    nz, cols = n // 4, out_width // n
    had = min(256, width)
    dma = pltpu.SemaphoreType.DMA
    vmem, hbm = pl.BlockSpec(memory_space=pltpu.VMEM), pl.BlockSpec(memory_space=pl.ANY)
    block = (count, cols)
    per_gather = [dma((nz,))] * 4 + [dma((nz, 2))] * 2
    hid_quant, projected = pl.pallas_call(
        functools.partial(kernel, n, group),
        out_shape=(
            jax.ShapeDtypeStruct((count, hidden), BF16),
            jax.ShapeDtypeStruct((count, out_width), BF16),
        ),
        in_specs=[vmem] * 4 + [hbm] * 3,
        out_specs=(vmem, hbm),
        scratch_shapes=[
            pltpu.VMEM(gate_up.shape, BF16),
            pltpu.VMEM(quant_codes.shape, BF16),
            pltpu.VMEM(down_rows.shape, BF16),
            pltpu.VMEM((count, width), BF16),
            pltpu.VMEM((count, width), BF16),
            pltpu.VMEM((count, hidden), BF16),
            pltpu.VMEM((count, out_width), BF16),
            pltpu.VMEM((nz, 2) + block, BF16),
            pltpu.VMEM((nz, 2) + block, BF16),
            pltpu.VMEM((nz,) + block, BF16),
            pltpu.VMEM((nz,) + block, BF16),
            pltpu.VMEM((nz,) + block, BF16),
            pltpu.VMEM((nz,) + block, BF16),
            dma((2, 4)),
            dma((2,)),
            dma,
            dma,
        ] + per_gather * 3,
        compiler_params=pltpu.CompilerParams(
            collective_id=0, has_side_effects=True, vmem_limit_bytes=62 * 2**20
        ),
        cost_estimate=pl.CostEstimate(
            flops=10 * count * width * hidden, bytes_accessed=50 * 2**20, transcendentals=0
        ),
    )(
        tokens, rotation_flip.reshape(1, width), jnp.asarray(hadamard_block(had), BF16),
        quant_exps, gate_up, quant_codes, down_rows,
    )
    gram = lax.dot_general(
        hid_quant, projected, (((0,), (0,)), ((), ())), preferred_element_type=F32
    )
    return (gram * (1.0 / count**0.5)).astype(BF16)


def solution(mesh):
    placed = (
        P(("dom", "tok"), None),
        P(),
        P("dom", None, "tok"),
        P("dom", None, "tok"),
        P("dom", None, "tok"),
        P(("dom", "tok"), None),
    )
    return jax.shard_map(
        functools.partial(per_device, mesh.shape["tok"]),
        mesh=mesh, in_specs=placed, out_specs=P(("dom", "tok"), None), check_vma=False,
    )
```

time: 203 us -> 89.2 us (0.44)
  blocking collectives: 95.8 us -> 0 us
  Pallas kernels: 0 us -> 81.4 us
  matrix products: 42.8 us -> 7.56 us
  waiting for transfers between devices: 31.1 us -> 0 us
  other arithmetic: 16.5 us -> 0 us
  between operations: 13.5 us -> 0.01 us
  local copies, waits for them, and re-layouts: 3.28 us -> 0 us
    psum x1 -> x0, blocking collectives: 95.8 us -> none  [per_device(): projected = lax.psum(partial_proj, 'tok').astype(jnp.bfloat16)]
    pallas_call x0 -> x1, Pallas kernels: none -> 81.4 us  [per_device(): pl.pallas_call(functools.partial(kernel, n, group), out_shape=(jax.ShapeD...]
    dot_general x6 -> x0, matrix products: 37 us -> none  [the longest x2 12.8 us: rotate(): jnp.einsum('ab,nbc,cd->nad', hadamard_table(outer_len), blocks, hadamard_...]
    all_gather x1 -> x0, waiting for transfers between devices: 30.4 us -> none  [per_device(): piece = lax.all_gather(tokens, 'tok', axis=0, tiled=True)]
    convert_element_type x2 -> x0, other arithmetic: 14.8 us -> none  [the longest x1 14.8 us: dequant(): (shaped * scales[:, :, None, :]).reshape(codes.shape).astype(jnp.bfloat16)]
    all_gather x1 -> x0, local copies, waits for them, and re-layouts: 3.27 us -> none  [per_device(): piece = lax.all_gather(tokens, 'tok', axis=0, tiled=True)]
  transfers between devices with their start and end apart: 1 -> 0, of which waited for: 1 -> 0; matrix products, arithmetic and copies ran while one was open for 8% -> 0% of each run, Pallas kernels for 0% -> 0%
where the time goes in v1:
time: 89.2 us; the launch traced here: 89 us
  Pallas kernels  81.4 us (91%)
  matrix products  7.56 us (8%)
    pallas_call x1, Pallas kernels, per_device(): pl.pallas_call(functools.partial(kernel, n, group), out_shape=(jax.ShapeD...  81.4 us
    dot_general x1, matrix products, per_device(): lax.dot_general(hid_quant, projected, (((0,), (0,)), ((), ())), preferred...  7.56 us

profile of v1, /device:TPU:1, one launch (start us, length us, event | category | flops | bytes accessed | tf_op | source)
XLA Modules:
  0.0 89.0 jit_solution(14322112214510922114)
XLA Ops:
  0.0 81.4 %shard_map.73 = (bf16[256,1024]{1,0:T(8,128)(2,1)}, bf16[256,4096]{1,0:T(8,128)(2,1)}) custom-call(bf16[16,4096]{1,0:T(8,128)(2,1)} %tok_ref.1, s32[1,4096]{1,0:T(1,128)} %bitcast.3, bf16[256,256]{1,0:T(8,128)(2,1)} %constant.4.clone.had_ref, s32[2,32,1024]{2,1,0:T(8,128)} %exps_ref.1, bf16[2,4096,1024]{2,1,0:T(8,128)(2,1)} %gu_hbm.1, ...), custom_call_target="tpu_custom_call" | custom-call | flops 10737418240 | bytes 52428800 | tf_op jit(solution)/shard_map/pallas_call | solution.py:265
  81.4 7.6 %multiply_convert_fusion = bf16[1024,4096]{1,0:T(8,128)(2,1)} fusion(bf16[256,1024]{1,0:T(8,128)(2,1)} %get-tuple-element.7, bf16[256,4096]{1,0:T(8,128)(2,1)} %get-tuple-element.8), kind=kOutput, calls=%fused_computation | convolution fusion | flops 2155872256 | bytes 11010048 | tf_op jit(solution)/shard_map/dot_general | solution.py:302

commit v2 on v1

--- a/solution.py
+++ b/solution.py
@@ -71,7 +71,7 @@
         pltpu.make_async_copy(gu_hbm.at[p], gu_v.at[p], gu_sem.at[p]) for p in range(2)
     ]
     down_copy = pltpu.make_async_copy(down_hbm, down_v, down_sem)
-    for copy in code_copies + gu_copies + [down_copy]:
+    for copy in code_copies:
         copy.start()
 
     def row_block(i):
@@ -156,6 +156,9 @@
     def between(k):
         for t in range(marks[k - 1] if k else 0, marks[k]):
             scale_chunk(t)
+        if k == 0:
+            for copy in gu_copies + [down_copy]:
+                copy.start()
 
     gather(row_block, (az_s, az_r, ay_s, ay_r, ac_s, ac_r), between, lambda i: None)
 
@@ -249,6 +252,15 @@
     for copy in sent:
         copy.wait_send()
     out_copy.wait()
+
+
+def gram_kernel(factor, hid_ref, proj_ref, out_ref, turned):
+    @pl.when(pl.program_id(0) == 0)
+    def _():
+        turned[...] = hid_ref[...].T
+
+    gram = jnp.dot(turned[...], proj_ref[...], preferred_element_type=F32)
+    out_ref[...] = (gram * factor).astype(BF16)
 
 
 def per_device(n, tokens, rotation_flip, gate_up, quant_codes, quant_exps, down_rows):
@@ -299,10 +311,19 @@
         tokens, rotation_flip.reshape(1, width), jnp.asarray(hadamard_block(had), BF16),
         quant_exps, gate_up, quant_codes, down_rows,
     )
-    gram = lax.dot_general(
-        hid_quant, projected, (((0,), (0,)), ((), ())), preferred_element_type=F32
-    )
-    return (gram * (1.0 / count**0.5)).astype(BF16)
+    lanes = min(512, out_width)
+    return pl.pallas_call(
+        functools.partial(gram_kernel, 1.0 / count**0.5),
+        out_shape=jax.ShapeDtypeStruct((hidden, out_width), BF16),
+        grid=(out_width // lanes,),
+        in_specs=[
+            pl.BlockSpec((count, hidden), lambda i: (0, 0)),
+            pl.BlockSpec((count, lanes), lambda i: (0, i)),
+        ],
+        out_specs=pl.BlockSpec((hidden, lanes), lambda i: (0, i)),
+        scratch_shapes=[pltpu.VMEM((hidden, count), BF16)],
+        compiler_params=pltpu.CompilerParams(vmem_limit_bytes=62 * 2**20),
+    )(hid_quant, projected)
 
 
 def solution(mesh):

time: 89.2 us -> 90.2 us (1.011)
  Pallas kernels: 81.4 us -> 89.9 us
  matrix products: 7.56 us -> 0 us
    pallas_call x0 -> x1, Pallas kernels: none -> 8.5 us  [per_device(): pl.pallas_call(functools.partial(gram_kernel, 1.0 / count ** 0.5), out_sh...]
    dot_general x1 -> x0, matrix products: 7.56 us -> none  [per_device(): lax.dot_general(hid_quant, projected, (((0,), (0,)), ((), ())), preferred...]
where the time goes in v2:
time: 90.2 us; the launch traced here: 89.9 us
  Pallas kernels  89.9 us (100%)
    pallas_call x1, Pallas kernels, per_device(): pl.pallas_call(functools.partial(kernel, n, group), out_shape=(jax.ShapeD...  81.4 us
    pallas_call x1, Pallas kernels, per_device(): pl.pallas_call(functools.partial(gram_kernel, 1.0 / count ** 0.5), out_sh...  8.5 us

profile of v2, /device:TPU:1, one launch (start us, length us, event | category | flops | bytes accessed | tf_op | source)
XLA Modules:
  0.0 89.9 jit_solution(3701444885945663855)
XLA Ops:
  0.0 81.4 %shard_map.73 = (bf16[256,1024]{1,0:T(8,128)(2,1)}, bf16[256,4096]{1,0:T(8,128)(2,1)}) custom-call(bf16[16,4096]{1,0:T(8,128)(2,1)} %tok_ref.1, s32[1,4096]{1,0:T(1,128)} %bitcast.1, bf16[256,256]{1,0:T(8,128)(2,1)} %constant.2.clone.had_ref, s32[2,32,1024]{2,1,0:T(8,128)} %exps_ref.1, bf16[2,4096,1024]{2,1,0:T(8,128)(2,1)} %gu_hbm.1, ...), custom_call_target="tpu_custom_call" | custom-call | flops 10737418240 | bytes 52428800 | tf_op jit(solution)/shard_map/pallas_call | solution.py:277
  81.4 8.5 %shard_map.74 = bf16[1024,4096]{1,0:T(8,128)(2,1)} custom-call(bf16[256,1024]{1,0:T(8,128)(2,1)} %get-tuple-element.7.hid_ref, bf16[256,4096]{1,0:T(8,128)(2,1)} %get-tuple-element.8.proj_ref), custom_call_target="tpu_custom_call" | custom-call | tf_op jit(solution)/shard_map/pallas_call | solution.py:315

commit v3 on v1

--- a/solution.py
+++ b/solution.py
@@ -71,7 +71,7 @@
         pltpu.make_async_copy(gu_hbm.at[p], gu_v.at[p], gu_sem.at[p]) for p in range(2)
     ]
     down_copy = pltpu.make_async_copy(down_hbm, down_v, down_sem)
-    for copy in code_copies + gu_copies + [down_copy]:
+    for copy in code_copies:
         copy.start()
 
     def row_block(i):
@@ -119,7 +119,7 @@
             send(block(i), block(i), c_s.at[k, 0], c_r.at[k, 0], c_peer)
             landed(i)
 
-        for k in range(nz - 1, 0, -1):
+        for k in range(1, nz):
             send(block(me), block(me), z_s.at[k], z_r.at[k], z_peer[k])
         out(0)
         between(0)
@@ -156,6 +156,9 @@
     def between(k):
         for t in range(marks[k - 1] if k else 0, marks[k]):
             scale_chunk(t)
+        if k == 0:
+            for copy in gu_copies + [down_copy]:
+                copy.start()
 
     gather(row_block, (az_s, az_r, ay_s, ay_r, ac_s, ac_r), between, lambda i: None)
 

time: 89.2 us -> 85.1 us (0.954)
  Pallas kernels: 81.4 us -> 77.4 us
    pallas_call x1, Pallas kernels: 81.4 us -> 77.4 us  [per_device(): pl.pallas_call(functools.partial(kernel, n, group), out_shape=(jax.ShapeD...]
where the time goes in v3:
time: 85.1 us; the launch traced here: 84.9 us
  Pallas kernels  77.4 us (91%)
  matrix products  7.55 us (9%)
    pallas_call x1, Pallas kernels, per_device(): pl.pallas_call(functools.partial(kernel, n, group), out_shape=(jax.ShapeD...  77.4 us
    dot_general x1, matrix products, per_device(): lax.dot_general(hid_quant, projected, (((0,), (0,)), ((), ())), preferred...  7.55 us

profile of v3, /device:TPU:1, one launch (start us, length us, event | category | flops | bytes accessed | tf_op | source)
XLA Modules:
  0.0 84.9 jit_solution(16195422715026554583)
XLA Ops:
  0.0 77.4 %shard_map.73 = (bf16[256,1024]{1,0:T(8,128)(2,1)}, bf16[256,4096]{1,0:T(8,128)(2,1)}) custom-call(bf16[16,4096]{1,0:T(8,128)(2,1)} %tok_ref.1, s32[1,4096]{1,0:T(1,128)} %bitcast.3, bf16[256,256]{1,0:T(8,128)(2,1)} %constant.4.clone.had_ref, s32[2,32,1024]{2,1,0:T(8,128)} %exps_ref.1, bf16[2,4096,1024]{2,1,0:T(8,128)(2,1)} %gu_hbm.1, ...), custom_call_target="tpu_custom_call" | custom-call | flops 10737418240 | bytes 52428800 | tf_op jit(solution)/shard_map/pallas_call | solution.py:268
  77.4 7.6 %multiply_convert_fusion = bf16[1024,4096]{1,0:T(8,128)(2,1)} fusion(bf16[256,1024]{1,0:T(8,128)(2,1)} %get-tuple-element.7, bf16[256,4096]{1,0:T(8,128)(2,1)} %get-tuple-element.8), kind=kOutput, calls=%fused_computation | convolution fusion | flops 2155872256 | bytes 11010048 | tf_op jit(solution)/shard_map/dot_general | solution.py:305
